TPU v7x, 32 devices: a whole 2x2x4 slice. The times are simulated.
32 devices in a mesh: ens: 2 (over x), tile: 8 (over z, y), comp: 2 (over core).
Axes of the slice: x: 2, y: 2, z: 4, core: 2. Of those that a mesh axis runs over, the one named last changes fastest.
Arguments:
- increment: bfloat16 [64, 128, 256], P(('ens', 'tile'), None, 'comp'), parts along dimension 0, may hold values from -6 to 6
- land_sea: int32 [32, 128], P('tile'), may hold values 0 or 1
- kernel_x: float32 [41, 256], P(None, 'comp'), may hold values from -1 to 1
- kernel_y: float32 [41, 256], P(None, 'comp'), may hold values from -1 to 1
- balance: bfloat16 [8, 256, 256], P('tile', 'comp'), may hold values from -0.375 to 0.375
Outputs:
- filtered: bfloat16 [64, 128, 256], P('ens', 'tile', 'comp'), parts along dimension 0
There are 2 independent parts, one for each index of `ens`. A program takes and returns all parts, laid end to end along the dimension named above; an argument that names none is the same for every part. Nothing has to cross between parts.
All inputs are finite; a program needn't handle non-finite values. No bound on the sum of `land_sea` on one device may be relied on, other than what follows from the above.
Results may differ from a plain program's by a relative error of at most 0.0057.
Values may be sent and summed in bfloat16 or wider, within the bound.
A program may use at most 64 MiB of HBM per device.

v0:
```python
import jax
import jax.numpy as jnp
from jax import lax
from jax.sharding import PartitionSpec as P


def zonal_filter(values, kernel):
    taps = kernel.shape[0]
    half_taps = (taps - 1) // 2
    total = jnp.zeros(values.shape, jnp.float32)
    for offset in range(taps):
        total = total + kernel[offset] * jnp.roll(values, half_taps - offset, axis=1)
    return total


def meridional_filter(values, kernel):
    taps = kernel.shape[0]
    half_taps = (taps - 1) // 2
    rows_all = values.shape[0]
    padded = jnp.pad(values, ((half_taps, half_taps), (0, 0), (0, 0)))
    total = jnp.zeros(values.shape, jnp.float32)
    for offset in range(taps):
        total = total + kernel[offset] * padded[offset : offset + rows_all]
    return total


def to_columns(row_bands):
    return lax.all_to_all(row_bands, "tile", split_axis=1, concat_axis=0, tiled=True)


def per_device(increment, land_sea, kernel_x, kernel_y, balance):
    sea = land_sea.astype(jnp.bfloat16)[:, :, None]
    masked = increment * sea
    zonal = (zonal_filter(masked, kernel_x) * sea.astype(jnp.float32)).astype(jnp.bfloat16)
    own_block = balance[0]
    mixed_rows = jnp.dot(
        lax.all_gather(zonal, "comp", axis=2, tiled=True),
        own_block.T,
        preferred_element_type=jnp.float32,
    )
    mixed = to_columns(mixed_rows.astype(jnp.bfloat16))
    return meridional_filter(mixed, kernel_y).astype(jnp.bfloat16)


def solution(mesh):
    return jax.shard_map(
        per_device,
        mesh=mesh,
        in_specs=(
            P(("ens", "tile"), None, "comp"),
            P("tile", None),
            P(None, "comp"),
            P(None, "comp"),
            P("tile", "comp", None),
        ),
        out_specs=P("ens", "tile", "comp"),
        check_vma=False,
    )
```

profile of v0, /device:TPU:0, one launch (start us, length us, event | category | flops | bytes accessed | tf_op | source)
XLA Modules:
  0.0 26.5 jit_solution(1189334224262708944)
XLA Ops:
  0.0 0.0 copy-start
  0.0 0.7 %fusion.1 = (f32[4,128]{1,0:T(4,128)S(1)}, bf16[4,128]{1,0:T(4,128)(2,1)S(1)}) fusion(s32[4,128]{1,0:T(4,128)} %param.6), kind=kLoop, calls=%fused_computation.127 | loop fusion | flops 1024 | bytes 5120 | tf_op jit(solution)/shard_map/convert_element_type | solution.py:34
  0.7 1.0 %broadcast_multiply_fusion = bf16[4,128,128]{2,1,0:T(8,128)(2,1)S(1)} fusion(bf16[4,128,128]{2,1,0:T(8,128)(2,1)} %param.5, bf16[4,128]{1,0:T(4,128)(2,1)S(1)} %get-tuple-element.6), kind=kLoop, calls=%fused_computation.44 | loop fusion | flops 65536 | bytes 263168 | tf_op jit(solution)/shard_map/mul | solution.py:33
  3.0 0.0 copy-start.2
  3.1 0.7 %copy-done.2 = f32[41,128]{1,0:T(8,128)S(1)} copy-done((f32[41,128]{1,0:T(8,128)S(1)}, f32[41,128]{1,0:T(8,128)}, u32[]{:S(2)}) %copy-start.2) | copy-done | bytes 21016
  3.8 0.0 copy-start.1
  3.8 0.9 %copy-done.1 = bf16[4,128,128]{2,1,0:T(8,128)(2,1)S(1)} copy-done((bf16[4,128,128]{2,1,0:T(8,128)(2,1)S(1)}, bf16[4,128,128]{2,1,0:T(8,128)(2,1)}, u32[]{:S(2)}) %copy-start.1) | copy-done | bytes 131096
  4.7 2.4 %multiply_convert_fusion = bf16[4,128,128]{2,1,0:T(8,128)(2,1)S(1)} fusion(bf16[4,108,128]{2,1,0:T(8,128)(2,1)S(1)} %get-tuple-element.8, bf16[4,20,128]{2,1,0:T(8,128)(2,1)S(1)} %get-tuple-element.10, bf16[4,109,128]{2,1,0:T(8,128)(2,1)S(1)} %get-tuple-element.12, bf16[4,19,128]{2,1,0:T(8,128)(2,1)S(1)} %get-tuple-element.14, ...), kind=kLoop, calls=%fused_computation.42 | loop fusion | flops 16187392 | bytes 5529088 | tf_op jit(solution)/shard_map/convert_element_type | solution.py:34
  7.1 2.1 %all_gather.3 = bf16[4,128,256]{2,1,0:T(8,128)(2,1)S(1)} all-gather(bf16[4,128,128]{2,1,0:T(8,128)(2,1)S(1)} %multiply_convert_fusion), channel_id=1, replica_groups=mesh['ens'=2,'tile'=8,'comp'=2] {'comp'}, dimensions={2}, use_global_device_ids=true | all-gather | bytes 393216 | tf_op jit(solution)/shard_map/all_gather | solution.py:37
  9.2 0.0 copy-done
  9.2 0.2 convolution_convert_fusion
  9.4 0.8 %copy.7 = bf16[4,128,128]{2,0,1:T(4,128)(2,1)} copy(bf16[4,128,128]{2,1,0:T(8,128)(2,1)S(1)} %convolution_convert_fusion) | data formatting | bytes 262144 | tf_op jit(solution)/shard_map/convert_element_type | solution.py:41
  10.2 0.0 copy-start.3
  10.2 7.3 %all-to-all-start = ((bf16[4,128,128]{2,0,1:T(4,128)(2,1)}), bf16[4,128,128]{2,0,1:T(4,128)(2,1)S(1)}, u32[]{:S(2)}, u32[]{:S(2)}) async-start(bf16[4,128,128]{2,0,1:T(4,128)(2,1)} %copy.7), calls=%async_computation | async-start | bytes 262144 | tf_op jit(solution)/shard_map/all_to_all | solution.py:28
  17.5 0.0 copy-done.3
  17.6 7.3 %all-to-all-done = bf16[4,128,128]{2,0,1:T(4,128)(2,1)S(1)} async-done(((bf16[4,128,128]{2,0,1:T(4,128)(2,1)}), bf16[4,128,128]{2,0,1:T(4,128)(2,1)S(1)}, u32[]{:S(2)}, u32[]{:S(2)}) %all-to-all-start) | async-done | bytes 131104 | tf_op jit(solution)/shard_map/all_to_all | solution.py:28
  24.9 1.6 %add_convert_fusion = bf16[32,16,128]{2,1,0:T(8,128)(2,1)} fusion(bf16[32,16,128]{2,1,0:T(8,128)(2,1)S(1)} %bitcast.174, f32[128]{0:T(128)S(1)} %get-tuple-element.126, f32[128]{0:T(128)S(1)} %get-tuple-element.127, f32[128]{0:T(128)S(1)} %get-tuple-element.88, f32[128]{0:T(128)S(1)} %get-tuple-element.89, f32[128]{0:T(128)S(1)} %get-tuple-element.90, ...), kind=kLoop, calls=%fused_computation.41 | loop fusion | flops 8060928 | bytes 283136 | tf_op jit(solution)/shard_map/convert_element_type | solution.py:42
  (47 shorter events, 1.1 us)
Async XLA Ops:
  0.0 9.2 %copy-start = (bf16[1,128,256]{2,1,0:T(8,128)(2,1)S(1)}, bf16[1,128,256]{2,1,0:T(8,128)(2,1)}, u32[]{:S(2)}) copy-start(bf16[1,128,256]{2,1,0:T(8,128)(2,1)} %param.9) | copy-start | bytes 196612
  3.0 0.7 %copy-start.2 = (f32[41,128]{1,0:T(8,128)S(1)}, f32[41,128]{1,0:T(8,128)}, u32[]{:S(2)}) copy-start(f32[41,128]{1,0:T(8,128)} %param.7) | copy-start | bytes 62980
  3.8 0.9 %copy-start.1 = (bf16[4,128,128]{2,1,0:T(8,128)(2,1)S(1)}, bf16[4,128,128]{2,1,0:T(8,128)(2,1)}, u32[]{:S(2)}) copy-start(bf16[4,128,128]{2,1,0:T(8,128)(2,1)} %param.5) | copy-start | bytes 393220
  10.2 7.3 %copy-start.3 = (f32[41,128]{1,0:T(8,128)S(1)}, f32[41,128]{1,0:T(8,128)}, u32[]{:S(2)}) copy-start(f32[41,128]{1,0:T(8,128)} %param.8) | copy-start | bytes 62980
  10.2 14.7 %all-to-all-start = ((bf16[4,128,128]{2,0,1:T(4,128)(2,1)}), bf16[4,128,128]{2,0,1:T(4,128)(2,1)S(1)}, u32[]{:S(2)}, u32[]{:S(2)}) async-start(bf16[4,128,128]{2,0,1:T(4,128)(2,1)} %copy.7), calls=%async_computation | async-start | bytes 262144 | tf_op jit(solution)/shard_map/all_to_all | solution.py:28
where the time goes:
time: 26.9 us; the launch traced here: 26.5 us
  starting transfers between devices  7.32 us (27%)
  waiting for transfers between devices  7.28 us (27%)
  other arithmetic  5.79 us (22%)
  local copies, waits for them, and re-layouts  3.41 us (13%)
  blocking collectives  2.09 us (8%)
  between operations  0.41 us (2%)
    all_to_all x1, starting transfers between devices, to_columns(): lax.all_to_all(row_bands, 'tile', split_axis=1, concat_axis=0, tiled=True)  7.32 us
    all_to_all x1, waiting for transfers between devices, to_columns(): lax.all_to_all(row_bands, 'tile', split_axis=1, concat_axis=0, tiled=True)  7.28 us
    convert_element_type x1, other arithmetic, per_device(): (zonal_filter(masked, kernel_x) * sea.astype(jnp.float32)).astype(jnp.bfl...  2.42 us
    all_gather x1, blocking collectives, per_device(): lax.all_gather(zonal, 'comp', axis=2, tiled=True)  2.09 us
    convert_element_type x1, other arithmetic, per_device(): return meridional_filter(mixed, kernel_y).astype(jnp.bfloat16)  1.63 us
    unnamed x8, local copies, waits for them, and re-layouts  1.54 us
    mul x1, other arithmetic, per_device(): masked = increment * sea  1.03 us
    slice x40, local copies, waits for them, and re-layouts, zonal_filter(): jnp.roll(values, half_taps - offset, axis=1)  1.03 us
  transfers between devices with their start and end apart: 1, of which 1 were waited for; matrix products, arithmetic and copies ran while one was open for 0% of the time, Pallas kernels for 0%

commit v1 on v0

v1 whole, which is shorter than its diff:
```python
import functools

import jax
import jax.numpy as jnp
from jax import lax
from jax.experimental import pallas as pl
from jax.experimental.pallas import tpu as pltpu
from jax.sharding import PartitionSpec as P

MESH = pl.DeviceIdType.MESH
F32 = jnp.float32
BF16 = jnp.bfloat16


def kernel(
    tiles, reach,
    inc_hbm, sea_hbm, kx_hbm, ky_hbm, bal_hbm, out_ref,
    inc, sea, kx, ky, bal, sea8, mask, nat, ext, zbuf, msend, mrecv, taps_y, acc,
    in_sem, zsend_sem, zrecv_sem, msend_sem, mrecv_sem,
):
    me = lax.axis_index("tile")
    core = lax.axis_index("comp")
    rows, columns, lanes = inc.shape
    half_x = columns // 2
    half = tiles // 2
    width = columns // tiles
    taps = kx.shape[0]
    reach_y = (taps - 1) // 2

    loads = [
        pltpu.make_async_copy(src, dst, in_sem.at[n])
        for n, (src, dst) in enumerate(
            ((sea_hbm, sea), (inc_hbm, inc), (kx_hbm, kx), (bal_hbm, bal), (ky_hbm, ky))
        )
    ]
    for load in loads:
        load.start()

    barrier = pltpu.get_barrier_semaphore()

    @pl.loop(1, tiles)
    def _(d):
        pl.semaphore_signal(
            barrier, inc=1, device_id={"tile": lax.rem(me + d, tiles)}, device_id_type=MESH
        )

    pl.semaphore_signal(barrier, inc=1, device_id={"comp": 1 - core}, device_id_type=MESH)

    loads[0].wait()
    sea8[...] = jnp.zeros_like(sea8)
    sea8[0:rows] = sea[...].astype(F32)
    row_of = lax.broadcasted_iota(jnp.int32, (8, lanes), 0)
    for r in range(rows):
        spread = lax.dot_general(
            sea8[...], (row_of == r).astype(F32), (((0,), (0,)), ((), ())),
            preferred_element_type=F32,
        )
        for h in range(2):
            mask[h * rows + r] = spread[h * half_x : (h + 1) * half_x]

    loads[1].wait()
    for r in range(rows):
        for h in range(2):
            j = h * rows + r
            nat[j] = inc[r, h * half_x : (h + 1) * half_x, :].astype(F32) * mask[j]
    for b in range(half_x // 8):
        ext[reach + 8 * b : reach + 8 * b + 8] = jnp.swapaxes(nat[:, 8 * b : 8 * b + 8, :], 0, 1)
    for i in range(reach):
        ext[i] = pltpu.roll(ext[i + half_x], rows, axis=0)
        ext[reach + half_x + i] = pltpu.roll(ext[reach + i], rows, axis=0)

    def chunk_of(step):
        return lax.rem(me + 1 + step, half)

    def exchange(q):
        return pltpu.make_async_remote_copy(
            src_ref=zbuf.at[q, core],
            dst_ref=zbuf.at[q, core],
            send_sem=zsend_sem.at[q],
            recv_sem=zrecv_sem.at[q],
            device_id={"comp": 1 - core},
            device_id_type=MESH,
        )

    def deliver(q, h):
        p = h * half + q
        return pltpu.make_async_remote_copy(
            src_ref=msend.at[q, h],
            dst_ref=mrecv.at[me],
            send_sem=msend_sem.at[p],
            recv_sem=mrecv_sem.at[me],
            device_id={"tile": p},
            device_id_type=MESH,
        )

    def zonal(q):
        base = pl.multiple_of(q * width, width)
        total = jnp.zeros((width, 8, lanes), F32)
        for k in range(taps):
            total = total + kx[k : k + 1, :][None] * ext[pl.ds(base + k, width)]
        cells = jnp.swapaxes(total, 0, 1) * mask[:, pl.ds(base, width), :]
        zbuf[q, core] = cells.astype(BF16)

    def finish(q):
        exchange(q).wait_recv()
        lhs = jnp.concatenate(
            [zbuf[q, c].reshape(8 * width, lanes) for c in range(2)], axis=-1
        )
        mixed = lax.dot_general(
            lhs, bal[0], (((1,), (1,)), ((), ())), preferred_element_type=F32
        )
        msend[q] = mixed.astype(BF16).reshape(2, rows, width, lanes)
        for h in range(2):
            p = h * half + q

            @pl.when(p == me)
            def _():
                mrecv[me] = msend[q, h]

            @pl.when(p != me)
            def _():
                deliver(q, h).start()

    loads[2].wait()
    zonal(chunk_of(0))
    pl.semaphore_wait(barrier, tiles)
    exchange(chunk_of(0)).start()
    loads[3].wait()

    @pl.loop(1, half)
    def _(step):
        q = chunk_of(step)
        zonal(q)
        exchange(q).start()
        finish(chunk_of(step - 1))

    finish(chunk_of(half - 1))

    loads[4].wait()
    acc[...] = jnp.zeros_like(acc)
    window = min(tiles, 2 * -(-reach_y // rows) + 1)
    near = window // 2 if window < tiles else 0
    margin = (taps_y.shape[0] - taps) // 2
    taps_y[...] = jnp.zeros_like(taps_y)
    for k in range(taps):
        taps_y[margin + k] = jnp.broadcast_to(ky[k : k + 1, :], (8, lanes))

    def gather(s):
        @pl.when(s != me)
        def _():
            pltpu.make_async_remote_copy(
                src_ref=mrecv.at[s],
                dst_ref=mrecv.at[s],
                send_sem=msend_sem.at[s],
                recv_sem=mrecv_sem.at[s],
                device_id={"tile": s},
                device_id_type=MESH,
            ).wait_recv()

        band = mrecv[s].astype(F32).reshape(rows, width // 8, 8, lanes)
        first = jnp.minimum(jnp.maximum(s - near, 0), tiles - window)
        for d in range(window):
            b = first + d
            start = rows * (s - b) + reach_y + margin
            for o in range(rows):
                y = rows * b + o
                total = acc[y]
                for i in range(rows):
                    total = total + taps_y[start + i - o][None] * band[i]
                acc[y] = total

    @pl.loop(0, half)
    def _(step):
        s = lax.rem(me + half - 1 - step + tiles, half)
        for h in range(2):
            gather(h * half + s)

    @pl.loop(0, tiles)
    def _(b):
        part = acc[pl.ds(rows * b, rows)]
        out_ref[pl.ds(rows * b, rows)] = part.reshape(rows, width, lanes).astype(BF16)

    @pl.loop(0, half)
    def _(q):
        exchange(q).wait_send()
        for h in range(2):
            @pl.when(h * half + q != me)
            def _():
                deliver(q, h).wait_send()


def per_device(tiles, increment, land_sea, kernel_x, kernel_y, balance):
    rows, columns, lanes = increment.shape
    taps = kernel_x.shape[0]
    reach = (taps - 1) // 2
    half_x, half, width = columns // 2, tiles // 2, columns // tiles
    ny = rows * tiles
    window = min(tiles, 2 * -(-reach // rows) + 1)
    margin = max(rows * (window - 1) + rows - 1 - reach, 0)
    vmem = pltpu.VMEM
    return pl.pallas_call(
        functools.partial(kernel, tiles, reach),
        out_shape=jax.ShapeDtypeStruct((ny, width, lanes), BF16),
        in_specs=[pl.BlockSpec(memory_space=pl.ANY)] * 5,
        out_specs=pl.BlockSpec(memory_space=pltpu.VMEM),
        scratch_shapes=[
            vmem(increment.shape, BF16),
            vmem(land_sea.shape, jnp.int32),
            vmem(kernel_x.shape, F32),
            vmem(kernel_y.shape, F32),
            vmem(balance.shape, BF16),
            vmem((8, columns), F32),
            vmem((2 * rows, half_x, lanes), F32),
            vmem((2 * rows, half_x, lanes), F32),
            vmem((half_x + 2 * reach, 8, lanes), F32),
            vmem((half, 2, 2 * rows, width, lanes), BF16),
            vmem((half, 2, rows, width, lanes), BF16),
            vmem((tiles, rows, width, lanes), BF16),
            vmem((taps + 2 * margin, 8, lanes), F32),
            vmem((ny, width // 8, 8, lanes), F32),
            pltpu.SemaphoreType.DMA((5,)),
            pltpu.SemaphoreType.DMA((half,)),
            pltpu.SemaphoreType.DMA((half,)),
            pltpu.SemaphoreType.DMA((tiles,)),
            pltpu.SemaphoreType.DMA((tiles,)),
        ],
        compiler_params=pltpu.CompilerParams(
            collective_id=0, has_side_effects=True, vmem_limit_bytes=48 * 1024 * 1024
        ),
    )(increment, land_sea, kernel_x, kernel_y, balance)


def solution(mesh):
    return jax.shard_map(
        functools.partial(per_device, mesh.shape["tile"]),
        mesh=mesh,
        in_specs=(
            P(("ens", "tile"), None, "comp"),
            P("tile", None),
            P(None, "comp"),
            P(None, "comp"),
            P("tile", "comp", None),
        ),
        out_specs=P("ens", "tile", "comp"),
        check_vma=False,
    )
```

time: 26.9 us -> 17.1 us (0.64)
  Pallas kernels: 0 us -> 12.2 us
  starting transfers between devices: 7.32 us -> 0 us
  waiting for transfers between devices: 7.28 us -> 0 us
  other arithmetic: 5.79 us -> 0 us
  blocking collectives: 2.09 us -> 0 us
  local copies, waits for them, and re-layouts: 3.41 us -> 4.56 us
  between operations: 0.41 us -> 0.01 us
    pallas_call x0 -> x1, Pallas kernels: none -> 12.2 us  [per_device(): pl.pallas_call(functools.partial(kernel, tiles, reach), out_shape=jax.Sha...]
    all_to_all x1 -> x0, starting transfers between devices: 7.32 us -> none  [to_columns(): lax.all_to_all(row_bands, 'tile', split_axis=1, concat_axis=0, tiled=True)]
    all_to_all x1 -> x0, waiting for transfers between devices: 7.28 us -> none  [to_columns(): lax.all_to_all(row_bands, 'tile', split_axis=1, concat_axis=0, tiled=True)]
    convert_element_type x3 -> x0, other arithmetic: 4.76 us -> none  [the longest x1 2.42 us: per_device(): (zonal_filter(masked, kernel_x) * sea.astype(jnp.float32)).astype(jnp.bfl...]
    unnamed x8 -> x11, local copies, waits for them, and re-layouts: 1.54 us -> 4.56 us
    all_gather x1 -> x0, blocking collectives: 2.09 us -> none  [per_device(): lax.all_gather(zonal, 'comp', axis=2, tiled=True)]
    mul x1 -> x0, other arithmetic: 1.03 us -> none  [per_device(): masked = increment * sea]
    slice x40 -> x0, local copies, waits for them, and re-layouts: 1.03 us -> none  [zonal_filter(): jnp.roll(values, half_taps - offset, axis=1)]
  transfers between devices with their start and end apart: 1 -> 0, of which waited for: 1 -> 0; matrix products, arithmetic and copies ran while one was open for 0% -> 0% of each run, Pallas kernels for 0% -> 0%
where the time goes in v1:
time: 17.1 us; the launch traced here: 16.8 us
  Pallas kernels  12.2 us (71%)
  local copies, waits for them, and re-layouts  4.56 us (27%)
    pallas_call x1, Pallas kernels, per_device(): pl.pallas_call(functools.partial(kernel, tiles, reach), out_shape=jax.Sha...  12.2 us
    unnamed x11, local copies, waits for them, and re-layouts  4.56 us

profile of v1, /device:TPU:0, one launch (start us, length us, event | category | flops | bytes accessed | tf_op | source)
XLA Modules:
  0.0 16.8 jit_solution(5910000677797578142)
XLA Ops:
  0.0 0.0 copy-start
  0.0 0.9 %copy-done = bf16[4,128,128]{2,1,0:T(8,128)(2,1)S(1)} copy-done((bf16[4,128,128]{2,1,0:T(8,128)(2,1)S(1)}, bf16[4,128,128]{2,1,0:T(8,128)(2,1)}, u32[]{:S(2)}) %copy-start) | copy-done | bytes 131096
  0.9 0.0 copy-start.1
  0.9 0.8 %copy-done.1 = bf16[1,128,256]{2,1,0:T(8,128)(2,1)S(1)} copy-done((bf16[1,128,256]{2,1,0:T(8,128)(2,1)S(1)}, bf16[1,128,256]{2,1,0:T(8,128)(2,1)}, u32[]{:S(2)}) %copy-start.1) | copy-done | bytes 65560
  1.7 0.0 copy-start.2
  1.7 0.7 %copy-done.2 = f32[41,128]{1,0:T(8,128)S(1)} copy-done((f32[41,128]{1,0:T(8,128)S(1)}, f32[41,128]{1,0:T(8,128)}, u32[]{:S(2)}) %copy-start.2) | copy-done | bytes 21016
  2.5 0.0 copy-start.3
  2.5 0.7 %copy-done.3 = f32[41,128]{1,0:T(8,128)S(1)} copy-done((f32[41,128]{1,0:T(8,128)S(1)}, f32[41,128]{1,0:T(8,128)}, u32[]{:S(2)}) %copy-start.3) | copy-done | bytes 21016
  3.2 0.0 copy-start.4
  3.2 0.7 %copy-done.4 = s32[4,128]{1,0:T(4,128)S(1)} copy-done((s32[4,128]{1,0:T(4,128)S(1)}, s32[4,128]{1,0:T(4,128)}, u32[]{:S(2)}) %copy-start.4) | copy-done | bytes 2072
  3.9 12.2 %shard_map.55 = bf16[32,16,128]{2,1,0:T(8,128)(2,1)S(1)} custom-call(bf16[4,128,128]{2,1,0:T(8,128)(2,1)S(1)} %copy-done, s32[4,128]{1,0:T(4,128)S(1)} %copy-done.4, f32[41,128]{1,0:T(8,128)S(1)} %copy-done.2, f32[41,128]{1,0:T(8,128)S(1)} %copy-done.3, bf16[1,128,256]{2,1,0:T(8,128)(2,1)S(1)} %copy-done.1), custom_call_target="tpu_custom_call" | custom-call | tf_op jit(solution)/shard_map/pallas_call | solution.py:201
  16.1 0.7 %copy.7 = bf16[32,16,128]{2,1,0:T(8,128)(2,1)} copy(bf16[32,16,128]{2,1,0:T(8,128)(2,1)S(1)} %shard_map.55) | data formatting | bytes 262144
Async XLA Ops:
  0.0 0.9 %copy-start = (bf16[4,128,128]{2,1,0:T(8,128)(2,1)S(1)}, bf16[4,128,128]{2,1,0:T(8,128)(2,1)}, u32[]{:S(2)}) copy-start(bf16[4,128,128]{2,1,0:T(8,128)(2,1)} %inc_hbm.1) | copy-start | bytes 393220
  0.9 0.8 %copy-start.1 = (bf16[1,128,256]{2,1,0:T(8,128)(2,1)S(1)}, bf16[1,128,256]{2,1,0:T(8,128)(2,1)}, u32[]{:S(2)}) copy-start(bf16[1,128,256]{2,1,0:T(8,128)(2,1)} %bal_hbm.1) | copy-start | bytes 196612
  1.7 0.7 %copy-start.2 = (f32[41,128]{1,0:T(8,128)S(1)}, f32[41,128]{1,0:T(8,128)}, u32[]{:S(2)}) copy-start(f32[41,128]{1,0:T(8,128)} %kx_hbm.1) | copy-start | bytes 62980
  2.5 0.7 %copy-start.3 = (f32[41,128]{1,0:T(8,128)S(1)}, f32[41,128]{1,0:T(8,128)}, u32[]{:S(2)}) copy-start(f32[41,128]{1,0:T(8,128)} %ky_hbm.1) | copy-start | bytes 62980
  3.2 0.7 %copy-start.4 = (s32[4,128]{1,0:T(4,128)S(1)}, s32[4,128]{1,0:T(4,128)}, u32[]{:S(2)}) copy-start(s32[4,128]{1,0:T(4,128)} %sea_hbm.1) | copy-start | bytes 6148

commit v2 on v1

--- a/solution.py
+++ b/solution.py
@@ -127,14 +127,20 @@
     exchange(chunk_of(0)).start()
     loads[3].wait()
 
-    @pl.loop(1, half)
+    lag = min(2, half - 1)
+    for step in range(1, lag):
+        zonal(chunk_of(step))
+        exchange(chunk_of(step)).start()
+
+    @pl.loop(lag, half)
     def _(step):
-        q = chunk_of(step)
-        zonal(q)
-        exchange(q).start()
-        finish(chunk_of(step - 1))
-
-    finish(chunk_of(half - 1))
+        zonal(chunk_of(step))
+        exchange(chunk_of(step)).start()
+        finish(chunk_of(step - lag))
+
+    @pl.loop(half - lag, half)
+    def _(step):
+        finish(chunk_of(step))
 
     loads[4].wait()
     acc[...] = jnp.zeros_like(acc)
@@ -201,7 +207,7 @@
     return pl.pallas_call(
         functools.partial(kernel, tiles, reach),
         out_shape=jax.ShapeDtypeStruct((ny, width, lanes), BF16),
-        in_specs=[pl.BlockSpec(memory_space=pl.ANY)] * 5,
+        in_specs=[pl.BlockSpec(memory_space=pltpu.HBM)] * 5,
         out_specs=pl.BlockSpec(memory_space=pltpu.VMEM),
         scratch_shapes=[
             vmem(increment.shape, BF16),
@@ -225,7 +231,7 @@
             pltpu.SemaphoreType.DMA((tiles,)),
         ],
         compiler_params=pltpu.CompilerParams(
-            collective_id=0, has_side_effects=True, vmem_limit_bytes=48 * 1024 * 1024
+            collective_id=0, has_side_effects=True, vmem_limit_bytes=63 * 1024 * 1024
         ),
     )(increment, land_sea, kernel_x, kernel_y, balance)
 

time: 17.1 us -> 14.2 us (0.83)
  local copies, waits for them, and re-layouts: 4.56 us -> 1.57 us
  Pallas kernels: 12.2 us -> 12.4 us
    unnamed x11 -> x1, local copies, waits for them, and re-layouts: 4.56 us -> 1.57 us
    pallas_call x1, Pallas kernels: 12.2 us -> 12.4 us  [per_device(): pl.pallas_call(functools.partial(kernel, tiles, reach), out_shape=jax.Sha...]
where the time goes in v2:
time: 14.2 us; the launch traced here: 14 us
  Pallas kernels  12.4 us (87%)
  local copies, waits for them, and re-layouts  1.57 us (11%)
    pallas_call x1, Pallas kernels, per_device(): pl.pallas_call(functools.partial(kernel, tiles, reach), out_shape=jax.Sha...  12.4 us
    unnamed x1, local copies, waits for them, and re-layouts  1.57 us

profile of v2, /device:TPU:0, one launch (start us, length us, event | category | flops | bytes accessed | tf_op | source)
XLA Modules:
  0.0 14.0 jit_solution(12587452728454891308)
XLA Ops:
  0.0 12.4 %shard_map.55 = bf16[32,16,128]{2,1,0:T(8,128)(2,1)} custom-call(bf16[4,128,128]{2,1,0:T(8,128)(2,1)} %inc_hbm.1, s32[4,128]{1,0:T(4,128)} %sea_hbm.1, f32[41,128]{1,0:T(8,128)} %kx_hbm.1, f32[41,128]{1,0:T(8,128)} %ky_hbm.1, bf16[1,128,256]{2,1,0:T(8,128)(2,1)} %bal_hbm.1), custom_call_target="tpu_custom_call" | custom-call | tf_op jit(solution)/shard_map/pallas_call | solution.py:207
  12.4 1.6 %copy.7 = bf16[32,16,128]{2,1,0:T(8,128)(2,1)} copy(bf16[32,16,128]{2,1,0:T(8,128)(2,1)} %shard_map.55) | data formatting | bytes 262144

commit v3 on v2

--- a/solution.py
+++ b/solution.py
@@ -231,9 +231,9 @@
             pltpu.SemaphoreType.DMA((tiles,)),
         ],
         compiler_params=pltpu.CompilerParams(
-            collective_id=0, has_side_effects=True, vmem_limit_bytes=63 * 1024 * 1024
+            collective_id=0, has_side_effects=True, vmem_limit_bytes=48 * 1024 * 1024
         ),
-    )(increment, land_sea, kernel_x, kernel_y, balance)
+    )(*(pltpu.with_memory_space_constraint(a, pltpu.HBM) for a in (increment, land_sea, kernel_x, kernel_y, balance)))
 
 
 def solution(mesh):

time: 14.2 us -> 12.6 us (0.89)
  local copies, waits for them, and re-layouts: 1.57 us -> 0.66 us
  Pallas kernels: 12.4 us -> 11.8 us
    unnamed x1, local copies, waits for them, and re-layouts: 1.57 us -> 0.66 us
    pallas_call x1, Pallas kernels: 12.4 us -> 11.8 us  [per_device(): pl.pallas_call(functools.partial(kernel, tiles, reach), out_shape=jax.Sha...]
where the time goes in v3:
time: 12.6 us; the launch traced here: 12.4 us
  Pallas kernels  11.8 us (94%)
  local copies, waits for them, and re-layouts  0.66 us (5%)
    pallas_call x1, Pallas kernels, per_device(): pl.pallas_call(functools.partial(kernel, tiles, reach), out_shape=jax.Sha...  11.8 us
    unnamed x1, local copies, waits for them, and re-layouts  0.66 us

profile of v3, /device:TPU:0, one launch (start us, length us, event | category | flops | bytes accessed | tf_op | source)
XLA Modules:
  0.0 12.4 jit_solution(15839946173379640261)
XLA Ops:
  0.0 11.8 %shard_map.55 = bf16[32,16,128]{2,1,0:T(8,128)(2,1)S(1)} custom-call(bf16[4,128,128]{2,1,0:T(8,128)(2,1)} %inc_hbm.1, s32[4,128]{1,0:T(4,128)} %sea_hbm.1, f32[41,128]{1,0:T(8,128)} %kx_hbm.1, f32[41,128]{1,0:T(8,128)} %ky_hbm.1, bf16[1,128,256]{2,1,0:T(8,128)(2,1)} %bal_hbm.1), custom_call_target="tpu_custom_call" | custom-call | tf_op jit(solution)/shard_map/pallas_call | solution.py:207
  11.8 0.7 %copy.7 = bf16[32,16,128]{2,1,0:T(8,128)(2,1)} copy(bf16[32,16,128]{2,1,0:T(8,128)(2,1)S(1)} %shard_map.55) | data formatting | bytes 262144

commit v4 on v3

--- a/solution.py
+++ b/solution.py
@@ -33,9 +33,6 @@
             ((sea_hbm, sea), (inc_hbm, inc), (kx_hbm, kx), (bal_hbm, bal), (ky_hbm, ky))
         )
     ]
-    for load in loads:
-        load.start()
-
     barrier = pltpu.get_barrier_semaphore()
 
     @pl.loop(1, tiles)
@@ -45,6 +42,9 @@
         )
 
     pl.semaphore_signal(barrier, inc=1, device_id={"comp": 1 - core}, device_id_type=MESH)
+
+    for load in loads:
+        load.start()
 
     loads[0].wait()
     sea8[...] = jnp.zeros_like(sea8)
@@ -95,10 +95,15 @@
 
     def zonal(q):
         base = pl.multiple_of(q * width, width)
-        total = jnp.zeros((width, 8, lanes), F32)
-        for k in range(taps):
-            total = total + kx[k : k + 1, :][None] * ext[pl.ds(base + k, width)]
-        cells = jnp.swapaxes(total, 0, 1) * mask[:, pl.ds(base, width), :]
+        parts = []
+        for g in range(0, width, 8):
+            seen = ext[pl.ds(base + g, 8 + taps - 1)]
+            total = jnp.zeros((8, 8, lanes), F32)
+            for k in range(taps):
+                total = total + kx[k : k + 1, :][None] * seen[k : k + 8]
+            cells = jnp.swapaxes(total, 0, 1)
+            parts.append(cells * mask[:, pl.ds(base + g, 8), :])
+        cells = jnp.concatenate(parts, axis=1)
         zbuf[q, core] = cells.astype(BF16)
 
     def finish(q):

time: 12.6 us -> 12.6 us (level)
  no operation moved by 1% of the time
where the time goes in v4:
time: 12.6 us; the launch traced here: 12.5 us
  Pallas kernels  11.8 us (94%)
  local copies, waits for them, and re-layouts  0.66 us (5%)
    pallas_call x1, Pallas kernels, per_device(): pl.pallas_call(functools.partial(kernel, tiles, reach), out_shape=jax.Sha...  11.8 us
    unnamed x1, local copies, waits for them, and re-layouts  0.66 us

profile of v4, /device:TPU:0, one launch (start us, length us, event | category | flops | bytes accessed | tf_op | source)
XLA Modules:
  0.0 12.5 jit_solution(12033298451086515939)
XLA Ops:
  0.0 11.8 %shard_map.55 = bf16[32,16,128]{2,1,0:T(8,128)(2,1)S(1)} custom-call(bf16[4,128,128]{2,1,0:T(8,128)(2,1)} %inc_hbm.1, s32[4,128]{1,0:T(4,128)} %sea_hbm.1, f32[41,128]{1,0:T(8,128)} %kx_hbm.1, f32[41,128]{1,0:T(8,128)} %ky_hbm.1, bf16[1,128,256]{2,1,0:T(8,128)(2,1)} %bal_hbm.1), custom_call_target="tpu_custom_call" | custom-call | tf_op jit(solution)/shard_map/pallas_call | solution.py:212
  11.8 0.7 %copy.7 = bf16[32,16,128]{2,1,0:T(8,128)(2,1)} copy(bf16[32,16,128]{2,1,0:T(8,128)(2,1)S(1)} %shard_map.55) | data formatting | bytes 262144

commit v5 on v3

--- a/solution.py
+++ b/solution.py
@@ -127,7 +127,7 @@
     exchange(chunk_of(0)).start()
     loads[3].wait()
 
-    lag = min(2, half - 1)
+    lag = min(1, half - 1)
     for step in range(1, lag):
         zonal(chunk_of(step))
         exchange(chunk_of(step)).start()

time: 12.6 us -> 12.6 us (level)
  no operation moved by 1% of the time
where the time goes in v5:
time: 12.6 us; the launch traced here: 12.4 us
  Pallas kernels  11.8 us (94%)
  local copies, waits for them, and re-layouts  0.66 us (5%)
    pallas_call x1, Pallas kernels, per_device(): pl.pallas_call(functools.partial(kernel, tiles, reach), out_shape=jax.Sha...  11.8 us
    unnamed x1, local copies, waits for them, and re-layouts  0.66 us

profile of v5, /device:TPU:0, one launch (start us, length us, event | category | flops | bytes accessed | tf_op | source)
XLA Modules:
  0.0 12.4 jit_solution(1293966225476950638)
XLA Ops:
  0.0 11.8 %shard_map.55 = bf16[32,16,128]{2,1,0:T(8,128)(2,1)S(1)} custom-call(bf16[4,128,128]{2,1,0:T(8,128)(2,1)} %inc_hbm.1, s32[4,128]{1,0:T(4,128)} %sea_hbm.1, f32[41,128]{1,0:T(8,128)} %kx_hbm.1, f32[41,128]{1,0:T(8,128)} %ky_hbm.1, bf16[1,128,256]{2,1,0:T(8,128)(2,1)} %bal_hbm.1), custom_call_target="tpu_custom_call" | custom-call | tf_op jit(solution)/shard_map/pallas_call | solution.py:207
  11.8 0.7 %copy.7 = bf16[32,16,128]{2,1,0:T(8,128)(2,1)} copy(bf16[32,16,128]{2,1,0:T(8,128)(2,1)S(1)} %shard_map.55) | data formatting | bytes 262144

commit v6 on v3

--- a/solution.py
+++ b/solution.py
@@ -52,7 +52,7 @@
     row_of = lax.broadcasted_iota(jnp.int32, (8, lanes), 0)
     for r in range(rows):
         spread = lax.dot_general(
-            sea8[...], (row_of == r).astype(F32), (((0,), (0,)), ((), ())),
+            sea8[...].astype(BF16), (row_of == r).astype(F32).astype(BF16), (((0,), (0,)), ((), ())),
             preferred_element_type=F32,
         )
         for h in range(2):

time: 12.6 us -> 12.6 us (level)
  no operation moved by 1% of the time
where the time goes in v6:
time: 12.6 us; the launch traced here: 12.4 us
  Pallas kernels  11.8 us (94%)
  local copies, waits for them, and re-layouts  0.66 us (5%)
    pallas_call x1, Pallas kernels, per_device(): pl.pallas_call(functools.partial(kernel, tiles, reach), out_shape=jax.Sha...  11.8 us
    unnamed x1, local copies, waits for them, and re-layouts  0.66 us

profile of v6, /device:TPU:0, one launch (start us, length us, event | category | flops | bytes accessed | tf_op | source)
XLA Modules:
  0.0 12.4 jit_solution(1529067300126031496)
XLA Ops:
  0.0 11.8 %shard_map.55 = bf16[32,16,128]{2,1,0:T(8,128)(2,1)S(1)} custom-call(bf16[4,128,128]{2,1,0:T(8,128)(2,1)} %inc_hbm.1, s32[4,128]{1,0:T(4,128)} %sea_hbm.1, f32[41,128]{1,0:T(8,128)} %kx_hbm.1, f32[41,128]{1,0:T(8,128)} %ky_hbm.1, bf16[1,128,256]{2,1,0:T(8,128)(2,1)} %bal_hbm.1), custom_call_target="tpu_custom_call" | custom-call | tf_op jit(solution)/shard_map/pallas_call | solution.py:207
  11.8 0.7 %copy.7 = bf16[32,16,128]{2,1,0:T(8,128)(2,1)} copy(bf16[32,16,128]{2,1,0:T(8,128)(2,1)S(1)} %shard_map.55) | data formatting | bytes 262144
